TPU v7x, 512 devices: a whole 4x4x16 slice. The times are simulated.
512 devices in a mesh: feat: 8 (over x, core), vert: 64 (over y, z).
Axes of the slice: x: 4, y: 4, z: 16, core: 2. Of those that a mesh axis runs over, the one named last changes fastest.
Arguments:
- features: bfloat16 [512, 131072], P('feat', 'vert'), may hold values from -6 to 6
- tiles: bfloat16 [64, 56, 128, 128], P('vert'), may hold values from -0.375 to 0.375
- tile_rows: int32 [64, 56], P('vert'), may hold values from 0 to 15, as said below
- tile_cols: int32 [64, 56], P('vert'), may hold values from 0 to 1023, as said below
- tile_counts: int32 [64], P('vert'), may hold values from 1 to 56, as said below
- weight: bfloat16 [512, 512], replicated, may hold values from -0.25 to 0.25
- output_gradient: bfloat16 [512, 131072], P(None, ('vert', 'feat')), may hold values from -6 to 6
Outputs:
- activation: bfloat16 [512, 131072], P(None, ('vert', 'feat'))
- weight_gradient: float32 [512, 512], replicated
- feature_grad: bfloat16 [512, 131072], P('feat', 'vert')
Inputs may be any that keep to these rules, and one draw needn't show every extreme that they name: `tile_rows`: slots at or beyond a block's count are unused; their tiles and indices are arbitrary. The block of a column tile, tile_cols // 16, equals the slot's own block or differs from it in exactly one of the lowest 4 bits. `tile_counts`: some block uses all 56 slots.
All inputs are finite; a program needn't handle non-finite values.
Results may differ from a plain program's by a relative error of at most 0.02.
Values may be sent and summed in bfloat16 or wider, within the bound.
A program may use at most 64 MiB of HBM per device.

v0:
```python
import jax
import jax.numpy as jnp
from jax import lax
from jax.sharding import PartitionSpec as P

LEVELS = 4


def partner(shard, axis, stride):
    return lax.ppermute(shard, axis, [(i, i ^ 1 << stride) for i in range(lax.axis_size(axis))])


def fetch_partners(features):
    fetched = []
    for bit in range(LEVELS):
        fetched.append(partner(features, "vert", bit))
    return fetched


def send_partials(remote_terms):
    received = []
    for bit in range(LEVELS):
        outgoing = remote_terms[:, bit].astype(jnp.bfloat16)
        received.append(partner(outgoing, "vert", bit).astype(jnp.float32))
    return received


def tile_products(stacked, level, local, rows, block_tiles, weights, row_tiles):
    picked = stacked[level, :, local]
    share_value = jnp.einsum(
        "cfk,crk->cfr", picked, block_tiles, preferred_element_type=jnp.float32
    )
    indicator_matrix = (rows[None, :] == jnp.arange(row_tiles, dtype=jnp.int32)[:, None]).astype(
        jnp.float32
    ) * weights[None, :]
    reduced_total = jnp.einsum("zy,yqw->qzw", indicator_matrix, share_value)
    return reduced_total.reshape(stacked.shape[1], row_tiles * stacked.shape[3])


def position_summands(share_value, slot_index, groups, feat_local, vdev):
    targets = jnp.arange(groups * (vdev // share_value.shape[2]), dtype=jnp.int32)
    placing = (slot_index[None, :] == targets[:, None]).astype(jnp.float32)
    return jnp.einsum("sc,cfk->fsk", placing, share_value).reshape(feat_local, groups, vdev)


def body(features, tiles, tile_rows, tile_cols, tile_counts, weight, output_gradient):
    feat_local, vdev = features.shape
    tile_side = tiles.shape[2]
    slot_count = tiles.shape[1]
    row_tiles = vdev // tile_side
    my_block = lax.axis_index("vert")
    block_tiles = tiles[0]
    rows = tile_rows[0]
    cols = tile_cols[0]
    differ = jnp.bitwise_xor(cols // row_tiles, my_block)
    level = jnp.zeros(cols.shape, jnp.int32)
    for bit in range(LEVELS):
        level = level + jnp.where(differ == 1 << bit, bit + 1, 0).astype(jnp.int32)
    local = cols % row_tiles
    valid = (jnp.arange(slot_count, dtype=jnp.int32) < tile_counts[0]).astype(jnp.float32)
    stacked = jnp.stack([features] + fetch_partners(features)).reshape(
        LEVELS + 1, feat_local, row_tiles, tile_side
    )
    aggregated = tile_products(stacked, level, local, rows, block_tiles, valid, row_tiles).astype(
        jnp.bfloat16
    )
    full_rows = lax.all_to_all(aggregated, "feat", split_axis=1, concat_axis=0, tiled=True)
    pre = jnp.einsum("io,iv->ov", weight, full_rows, preferred_element_type=jnp.float32)
    sigma = jax.nn.sigmoid(pre)
    activation = (pre * sigma).astype(jnp.bfloat16)
    pre_grad = (output_gradient.astype(jnp.float32) * sigma * (1.0 + pre * (1.0 - sigma))).astype(
        jnp.bfloat16
    )
    weight_term = jnp.einsum("iv,ov->io", full_rows, pre_grad, preferred_element_type=jnp.float32)
    weight_gradient = lax.psum(weight_term, ("feat", "vert"))
    agg_grad = jnp.einsum("io,ov->iv", weight, pre_grad, preferred_element_type=jnp.float32).astype(
        jnp.bfloat16
    )
    grad_cols = lax.all_to_all(agg_grad, "feat", split_axis=0, concat_axis=1, tiled=True)
    picked = grad_cols.reshape(feat_local, row_tiles, tile_side)[:, rows, :]
    share_value = (
        jnp.einsum("fcr,crk->cfk", picked, block_tiles, preferred_element_type=jnp.float32)
        * valid[:, None, None]
    )
    spread = position_summands(share_value, level * row_tiles + local, LEVELS + 1, feat_local, vdev)
    received = send_partials(spread[:, 1:])
    feature_grad = spread[:, 0]
    for term in received:
        feature_grad = feature_grad + term
    return (activation, weight_gradient, feature_grad.astype(jnp.bfloat16))


def solution(mesh):
    in_specs = (
        P("feat", "vert"),
        P("vert", None, None, None),
        P("vert", None),
        P("vert", None),
        P("vert"),
        P(),
        P(None, ("vert", "feat")),
    )
    out_specs = (P(None, ("vert", "feat")), P(), P("feat", "vert"))
    return jax.shard_map(body, mesh=mesh, in_specs=in_specs, out_specs=out_specs, check_vma=False)
```

profile of v0, /device:TPU:1, one launch (start us, length us, event | category | flops | bytes accessed | tf_op | source)
XLA Modules:
  0.0 628.8 jit_solution(14471863540489969215)
XLA Ops:
  7.2 5.9 collective-permute-start.1
  13.1 3.5 collective-permute-start
  16.6 12.7 %collective-permute-start.3 = (bf16[64,2048]{1,0:T(8,128)(2,1)}, bf16[64,2048]{1,0:T(8,128)(2,1)S(1)}, u32[]{:S(2)}, u32[]{:S(2)}) collective-permute-start(bf16[64,2048]{1,0:T(8,128)(2,1)} %param.7), channel_id=1, source_target_pairs={{0,8},{1,9},{2,10},{3,11},{4,12},{5,13},{6,14},{7,15},{8,0},{9,1},... | collective-permute-start | bytes 786440 | tf_op jit(solution)/shard_map/ppermute | solution.py:10
  29.4 4.0 collective-permute-start.2
  34.0 0.7 fusion.49
  34.7 1.0 copy.87
  35.7 0.8 copy_dynamic-update-slice_fusion.4
  36.6 10.2 %collective-permute-done.3 = bf16[64,2048]{1,0:T(8,128)(2,1)S(1)} collective-permute-done((bf16[64,2048]{1,0:T(8,128)(2,1)}, bf16[64,2048]{1,0:T(8,128)(2,1)S(1)}, u32[]{:S(2)}, u32[]{:S(2)}) %collective-permute-start.3) | collective-permute-done | bytes 262176 | tf_op jit(solution)/shard_map/ppermute | solution.py:10
  46.9 31.9 %collective-permute-done.2 = bf16[64,2048]{1,0:T(8,128)(2,1)S(1)} collective-permute-done((bf16[64,2048]{1,0:T(8,128)(2,1)}, bf16[64,2048]{1,0:T(8,128)(2,1)S(1)}, u32[]{:S(2)}, u32[]{:S(2)}) %collective-permute-start.2) | collective-permute-done | bytes 262176 | tf_op jit(solution)/shard_map/ppermute | solution.py:10
  78.8 0.8 copy_dynamic-update-slice_fusion.3
  79.5 0.8 copy_dynamic-update-slice_fusion.2
  80.3 0.8 copy_dynamic-update-slice_fusion.1
  81.0 0.8 copy_dynamic-update-slice_fusion
  81.8 2.2 gather_fusion
  84.1 1.4 fusion.2
  85.4 0.6 fusion.18
  86.0 0.1 convert_element_type.72
  86.1 0.8 copy.75
  86.9 4.8 all-to-all-start
  91.7 0.1 copy.76
  91.8 6.3 %all-to-all-done = bf16[64,8,256]{2,0,1:T(8,128)(2,1)S(1)} async-done(((bf16[64,8,256]{2,0,1:T(8,128)(2,1)}), bf16[64,8,256]{2,0,1:T(8,128)(2,1)S(1)}, u32[]{:S(2)}, u32[]{:S(2)}) %all-to-all-start) | async-done | bytes 262176 | tf_op jit(solution)/shard_map/all_to_all | solution.py:67
  98.2 1.2 multiply_convert_fusion
  99.4 0.3 fusion.17
  99.7 0.8 copy.77
  100.6 4.4 all-to-all-start.1
  105.0 6.5 %all-to-all-done.1 = bf16[8,64,256]{2,1,0:T(8,128)(2,1)S(1)} async-done(((bf16[8,64,256]{2,1,0:T(8,128)(2,1)}), bf16[8,64,256]{2,1,0:T(8,128)(2,1)S(1)}, u32[]{:S(2)}, u32[]{:S(2)}) %all-to-all-start.1) | async-done | bytes 262176 | tf_op jit(solution)/shard_map/all_to_all | solution.py:79
  111.5 0.1 copy.78
  111.6 0.1 reshape.231
  111.8 0.7 gather_fusion.1
  112.5 0.6 fusion.11
  113.1 2.4 fusion.8
  115.5 4.4 reshape.232
  119.9 2.5 convert.6
  122.4 1.9 fusion.51
  124.3 0.2 copy.115
  124.5 0.2 copy.112
  124.6 0.9 copy.113
  125.5 0.9 copy.114
  126.3 1.9 collective-permute-start.5
  128.3 1.9 collective-permute-start.6
  130.2 8.5 %collective-permute-start.7 = (bf16[64,2048]{1,0:T(8,128)(2,1)S(1)}, bf16[64,2048]{1,0:T(8,128)(2,1)}, u32[]{:S(2)}, u32[]{:S(2)}) collective-permute-start(bf16[64,2048]{1,0:T(8,128)(2,1)S(1)} %bitcast.108), channel_id=1, source_target_pairs={{0,8},{1,9},{2,10},{3,11},{4,12},{5,13},{6,14},{7,15},{8,0},{9,1},... | collective-permute-start | bytes 786440 | tf_op jit(solution)/shard_map/ppermute | solution.py:10
  138.7 5.8 collective-permute-start.4
  144.5 1.3 fusion.52
  145.8 1.8 copy.81
  147.7 33.5 %collective-permute-done.6 = bf16[64,2048]{1,0:T(8,128)(2,1)} collective-permute-done((bf16[64,2048]{1,0:T(8,128)(2,1)}, bf16[64,2048]{1,0:T(8,128)(2,1)}, u32[]{:S(2)}, u32[]{:S(2)}) %collective-permute-start.6) | collective-permute-done | bytes 262176 | tf_op jit(solution)/shard_map/ppermute | solution.py:10
  181.2 2.2 fusion.25
  183.3 436.4 %all-reduce.2.cloned.1.call-done = f32[512,512]{1,0:T(8,128)} async-done(((f32[512,512]{1,0:T(8,128)}), f32[512,512]{1,0:T(8,128)}) %all-reduce.2.cloned.1.call-update) | async-done | bytes 1048592 | tf_op jit(solution)/shard_map/psum | solution.py:75
  619.7 2.3 copy.122
  (28 shorter events, 0.3 us)
Async XLA Ops:
  7.2 76.9 %copy-start = (bf16[1,56,128,128]{3,2,1,0:T(8,128)(2,1)S(1)}, bf16[1,56,128,128]{3,2,1,0:T(8,128)(2,1)}, u32[]{:S(2)}) copy-start(bf16[1,56,128,128]{3,2,1,0:T(8,128)(2,1)} %param.8) | copy-start | bytes 5505028
  7.2 29.3 %collective-permute-start.1 = (bf16[64,2048]{1,0:T(8,128)(2,1)}, bf16[64,2048]{1,0:T(8,128)(2,1)S(1)}, u32[]{:S(2)}, u32[]{:S(2)}) collective-permute-start(bf16[64,2048]{1,0:T(8,128)(2,1)} %param.7), channel_id=1, source_target_pairs={{0,2},{1,3},{2,0},{3,1},{4,6},{5,7},{6,4},{7,5},{8,10},{9,11},{10,... | collective-permute-start | bytes 786440 | tf_op jit(solution)/shard_map/ppermute | solution.py:10
  13.1 23.5 %collective-permute-start = (bf16[64,2048]{1,0:T(8,128)(2,1)}, bf16[64,2048]{1,0:T(8,128)(2,1)S(1)}, u32[]{:S(2)}, u32[]{:S(2)}) collective-permute-start(bf16[64,2048]{1,0:T(8,128)(2,1)} %param.7), channel_id=1, source_target_pairs={{0,1},{1,0},{2,3},{3,2},{4,5},{5,4},{6,7},{7,6},{8,9},{9,8},{10,11... | collective-permute-start | bytes 786440 | tf_op jit(solution)/shard_map/ppermute | solution.py:10
  16.6 30.2 %collective-permute-start.3 = (bf16[64,2048]{1,0:T(8,128)(2,1)}, bf16[64,2048]{1,0:T(8,128)(2,1)S(1)}, u32[]{:S(2)}, u32[]{:S(2)}) collective-permute-start(bf16[64,2048]{1,0:T(8,128)(2,1)} %param.7), channel_id=1, source_target_pairs={{0,8},{1,9},{2,10},{3,11},{4,12},{5,13},{6,14},{7,15},{8,0},{9,1},... | collective-permute-start | bytes 786440 | tf_op jit(solution)/shard_map/ppermute | solution.py:10
  29.4 49.4 %collective-permute-start.2 = (bf16[64,2048]{1,0:T(8,128)(2,1)}, bf16[64,2048]{1,0:T(8,128)(2,1)S(1)}, u32[]{:S(2)}, u32[]{:S(2)}) collective-permute-start(bf16[64,2048]{1,0:T(8,128)(2,1)} %param.7), channel_id=1, source_target_pairs={{0,4},{1,5},{2,6},{3,7},{4,0},{5,1},{6,2},{7,3},{8,12},{9,13},{10,... | collective-permute-start | bytes 786440 | tf_op jit(solution)/shard_map/ppermute | solution.py:10
  84.0 1.4 copy-start.3
  85.4 6.2 copy-start.2
  86.0 12.1 %copy-start.1 = (bf16[512,512]{1,0:T(8,128)(2,1)S(1)}, bf16[512,512]{1,0:T(8,128)(2,1)}, u32[]{:S(2)}) copy-start(bf16[512,512]{1,0:T(8,128)(2,1)} %param.12) | copy-start | bytes 1572868
  86.9 11.3 %all-to-all-start = ((bf16[64,8,256]{2,0,1:T(8,128)(2,1)}), bf16[64,8,256]{2,0,1:T(8,128)(2,1)S(1)}, u32[]{:S(2)}, u32[]{:S(2)}) async-start(bf16[64,8,256]{2,0,1:T(8,128)(2,1)} %copy.75), calls=%async_computation | async-start | bytes 524288 | tf_op jit(solution)/shard_map/all_to_all | solution.py:67
  99.4 5.6 copy-start.4
  100.6 10.9 %all-to-all-start.1 = ((bf16[8,64,256]{2,1,0:T(8,128)(2,1)}), bf16[8,64,256]{2,1,0:T(8,128)(2,1)S(1)}, u32[]{:S(2)}, u32[]{:S(2)}) async-start(bf16[8,64,256]{2,1,0:T(8,128)(2,1)} %bitcast.12), calls=%async_computation.1 | async-start | bytes 524288 | tf_op jit(solution)/shard_map/all_to_all | solution.py:79
  104.9 514.8 %all-reduce.2.cloned.1.call-start = ((), (), s32[]{:S(2)}) async-start(), calls=%async_computation.2 | async-start | bytes 2097152 | tf_op jit(solution)/shard_map/psum | solution.py:75
  126.3 21.3 %collective-permute-start.5 = (bf16[64,2048]{1,0:T(8,128)(2,1)}, bf16[64,2048]{1,0:T(8,128)(2,1)}, u32[]{:S(2)}, u32[]{:S(2)}) collective-permute-start(bf16[64,2048]{1,0:T(8,128)(2,1)} %bitcast.96), channel_id=1, source_target_pairs={{0,2},{1,3},{2,0},{3,1},{4,6},{5,7},{6,4},{7,5},{8,10},{9,11},{10,... | collective-permute-start | bytes 786440 | tf_op jit(solution)/shard_map/ppermute | solution.py:10
  128.3 52.9 %collective-permute-start.6 = (bf16[64,2048]{1,0:T(8,128)(2,1)}, bf16[64,2048]{1,0:T(8,128)(2,1)}, u32[]{:S(2)}, u32[]{:S(2)}) collective-permute-start(bf16[64,2048]{1,0:T(8,128)(2,1)} %bitcast.95), channel_id=1, source_target_pairs={{0,4},{1,5},{2,6},{3,7},{4,0},{5,1},{6,2},{7,3},{8,12},{9,13},{10,... | collective-permute-start | bytes 786440 | tf_op jit(solution)/shard_map/ppermute | solution.py:10
  130.2 50.9 %collective-permute-start.7 = (bf16[64,2048]{1,0:T(8,128)(2,1)S(1)}, bf16[64,2048]{1,0:T(8,128)(2,1)}, u32[]{:S(2)}, u32[]{:S(2)}) collective-permute-start(bf16[64,2048]{1,0:T(8,128)(2,1)S(1)} %bitcast.108), channel_id=1, source_target_pairs={{0,8},{1,9},{2,10},{3,11},{4,12},{5,13},{6,14},{7,15},{8,0},{9,1},... | collective-permute-start | bytes 786440 | tf_op jit(solution)/shard_map/ppermute | solution.py:10
  138.7 42.4 %collective-permute-start.4 = (bf16[64,2048]{1,0:T(8,128)(2,1)S(1)}, bf16[64,2048]{1,0:T(8,128)(2,1)}, u32[]{:S(2)}, u32[]{:S(2)}) collective-permute-start(bf16[64,2048]{1,0:T(8,128)(2,1)S(1)} %bitcast.107), channel_id=1, source_target_pairs={{0,1},{1,0},{2,3},{3,2},{4,5},{5,4},{6,7},{7,6},{8,9},{9,8},{10,11... | collective-permute-start | bytes 786440 | tf_op jit(solution)/shard_map/ppermute | solution.py:10
  145.8 35.3 %slice-start = ((f32[64,5,2048]{2,1,0:T(8,128)}), f32[64,1,2048]{2,1,0:T(1,128)S(1)}, s32[]{:S(2)}) async-start(f32[64,5,2048]{2,1,0:T(8,128)} %reshape.232), calls=%async_computation.3 | async-start | bytes 1048576 | tf_op jit(solution)/shard_map/slice | solution.py:87
Sparse Core Ops, SparseCore 0:
  146.0 473.7 all-reduce.1
where the time goes:
time: 630 us; the launch traced here: 629 us
  waiting for transfers between devices  525 us (83%)
  starting transfers between devices  53.5 us (8%)
  local copies, waits for them, and re-layouts  22.5 us (4%)
  between operations  14.9 us (2%)
  matrix products  7.74 us (1%)
    psum x1, waiting for transfers between devices, body(): weight_gradient = lax.psum(weight_term, ('feat', 'vert'))  436 us
    ppermute x8, waiting for transfers between devices, partner(): lax.ppermute(shard, axis, [(i, i ^ 1 << stride) for i in range(lax.axis_s...  75.5 us
    ppermute x8, starting transfers between devices, partner(): lax.ppermute(shard, axis, [(i, i ^ 1 << stride) for i in range(lax.axis_s...  44.3 us
  transfers between devices with their start and end apart: 11, of which 6 were waited for; matrix products, arithmetic and copies ran while one was open for 1% of the time, Pallas kernels for 0%

commit v1 on v0

v1 whole, which is shorter than its diff:
```python
import functools

import jax
import jax.numpy as jnp
from jax import lax
from jax.experimental import pallas as pl
from jax.experimental.pallas import tpu as pltpu
from jax.sharding import PartitionSpec as P

NZ = 16
LEVELS = 4
CHUNKS = 4
GROUP = 8
MESH = pl.DeviceIdType.MESH
BF16, F32 = jnp.bfloat16, jnp.float32
NT = (((1,), (1,)), ((), ()))


def offsets(slots, row_tiles):
    sizes = (slots, slots, slots, slots, row_tiles, (LEVELS + 1) * row_tiles)
    starts = [0]
    for size in sizes:
        starts.append(starts[-1] + size)
    return starts


def index_kernel(slots, row_tiles, rows_ref, cols_ref, count_ref, out_ref):
    src, row, prev_f, prev_b, last_f, last_b, end = offsets(slots, row_tiles)
    block = lax.axis_index("vert")
    count = count_ref[0]

    def clear(i, carry):
        out_ref[last_f + i] = jnp.int32(slots)
        return carry

    lax.fori_loop(0, end - last_f, clear, 0)

    def step(c, carry):
        valid = c < count
        col = cols_ref[0, c]
        differ = (col // row_tiles) ^ block
        level = jnp.int32(0)
        for bit in range(LEVELS):
            level = level + jnp.where(differ >= (1 << bit), 1, 0).astype(jnp.int32)
        tile = jnp.where(valid, level * row_tiles + col % row_tiles, 0)
        line = jnp.where(valid, rows_ref[0, c], 0)
        out_ref[src + c] = tile
        out_ref[row + c] = line
        before = out_ref[last_f + line]
        out_ref[prev_f + c] = before
        out_ref[last_f + line] = jnp.where(valid, c, before)
        before = out_ref[last_b + tile]
        out_ref[prev_b + c] = before
        out_ref[last_b + tile] = jnp.where(valid, c, before)
        return carry

    lax.fori_loop(0, slots, step, 0)


def layer_kernel(
    nf, ny, slots, row_tiles, tile,
    idx, feat, tiles, weight, out_grad,
    act, wgrad, fgrad,
    stk, acc, wt, agg, full, pg, ag, gc, wgs, frs, red, yr, zs, zr, zsum, zh, zag, yag,
    part, rly, mrg, rv, ssem, rsem,
):
    src, row, prev_f, prev_b, last_f, last_b, _ = offsets(slots, row_tiles)
    fl = feat.shape[0]
    f_all = nf * fl
    per = row_tiles // nf
    me_f, me_v = lax.axis_index("feat"), lax.axis_index("vert")
    z, y = me_v % NZ, me_v // NZ
    zl, zhi = z % 4, z // 4
    piece = row_tiles // CHUNKS

    used = [0]

    def send(source, dest, f, v):
        n = used[0]
        used[0] += 1
        copy = pltpu.make_async_remote_copy(
            source, dest, ssem.at[n], rsem.at[n], device_id=(f, v), device_id_type=MESH
        )
        copy.start()
        return copy

    peers = [(me_f ^ d, me_v) for d in range(1, nf)]
    peers += [(me_f, me_v ^ d) for d in (1, 2, 3, 4, 8, 12)]
    peers += [(me_f, (y ^ d) * NZ + z) for d in range(1, ny)]
    barrier = pltpu.get_barrier_semaphore()
    for f, v in peers:
        pl.semaphore_signal(barrier, inc=1, device_id=(f, v), device_id_type=MESH)
    for t in range(row_tiles):
        stk[t] = feat[:, t * tile : (t + 1) * tile]
    pl.semaphore_wait(barrier, len(peers))

    def rows_of(level, k):
        return pl.ds(level * row_tiles + k * piece, piece)

    waits = []
    first = [
        send(stk.at[rows_of(0, k)], stk.at[rows_of(3, k)], me_f, me_v ^ 4) for k in range(CHUNKS)
    ]
    for bit in (1, 0):
        waits.append(
            send(
                stk.at[pl.ds(0, row_tiles)],
                stk.at[pl.ds((bit + 1) * row_tiles, row_tiles)],
                me_f,
                me_v ^ (1 << bit),
            )
        )
    acc[slots] = jnp.zeros(acc.shape[1:], F32)
    wt[...] = weight[...].astype(F32).T.astype(BF16)
    for k, copy in enumerate(first):
        copy.wait()
        waits.append(send(stk.at[rows_of(3, k)], stk.at[rows_of(4, k)], me_f, me_v ^ 12))
    for copy in waits:
        copy.wait()

    def forward(g, carry):
        products = []
        for u in range(GROUP):
            c = g * GROUP + u
            picked = stk[idx[src + c]]
            products.append(
                lax.dot_general(picked, tiles[c], NT, preferred_element_type=F32)
            )
        for u in range(GROUP):
            c = g * GROUP + u
            acc[c] = products[u] + acc[idx[prev_f + c]]
        return carry

    lax.fori_loop(0, slots // GROUP, forward, 0)

    for r in range(row_tiles):
        k = r % per
        agg[r // per, :, k * tile : (k + 1) * tile] = acc[idx[last_f + r]].astype(BF16)
    full[me_f] = agg[me_f]
    waits = []
    for d in range(1, nf):
        waits.append(send(agg.at[me_f ^ d], full.at[me_f], me_f ^ d, me_v))
    for copy in waits:
        copy.wait()

    share = per * tile
    rows = full[...].reshape(f_all, share)
    halves = 2
    h = f_all // halves
    for i in range(halves):
        part_rows = slice(i * h, (i + 1) * h)
        pre = jnp.dot(wt[part_rows, :], rows, preferred_element_type=F32)
        sigma = jax.nn.sigmoid(pre)
        act[part_rows, :] = (pre * sigma).astype(BF16)
        pg[part_rows, :] = (
            out_grad[part_rows, :].astype(F32) * sigma * (1.0 + pre * (1.0 - sigma))
        ).astype(BF16)
    grads = pg[...]
    for i in range(halves):
        part_rows = slice(i * h, (i + 1) * h)
        agg_grad = jnp.dot(weight[part_rows, :], grads, preferred_element_type=F32).astype(BF16)
        for k in range(per):
            ag[i * nf // halves : (i + 1) * nf // halves, k] = agg_grad[
                :, k * tile : (k + 1) * tile
            ].reshape(nf // halves, fl, tile)
    back = []
    mine = pl.ds(me_f * per, per)
    for d in range(1, nf):
        back.append(send(ag.at[me_f ^ d], gc.at[mine], me_f ^ d, me_v))
    gc[mine] = ag[me_f]
    for j in range(nf):
        wgs[j] = lax.dot_general(full[j], pg[...], NT, preferred_element_type=F32).astype(BF16)
    terms = [send(wgs.at[me_f ^ d], frs.at[me_f], me_f ^ d, me_v) for d in range(1, nf)]
    frs[me_f] = wgs[me_f]
    for copy in back:
        copy.wait()

    def backward(g, carry):
        products = []
        for u in range(GROUP):
            c = g * GROUP + u
            picked = gc[idx[row + c]]
            products.append(jnp.dot(picked, tiles[c], preferred_element_type=F32))
        for u in range(GROUP):
            c = g * GROUP + u
            acc[c] = products[u] + acc[idx[prev_b + c]]
        return carry

    lax.fori_loop(0, slots // GROUP, backward, 0)

    def summed(level, t):
        return acc[idx[last_b + level * row_tiles + t]]

    waits, relayed = [], []
    for k in range(CHUNKS):
        for t in range(k * piece, (k + 1) * piece):
            part[2, t] = summed(4, t).astype(BF16)
        span = pl.ds(k * piece, piece)
        relayed.append(send(part.at[2, span], rly.at[span], me_f, me_v ^ 12))
    for bit in (1, 0):
        for t in range(row_tiles):
            part[bit, t] = summed(bit + 1, t).astype(BF16)
        waits.append(send(part.at[bit], rv.at[bit], me_f, me_v ^ (1 << bit)))

    merged = []

    def relay(k):
        relayed[k].wait()
        for t in range(k * piece, (k + 1) * piece):
            mrg[t] = (summed(3, t) + rly[t].astype(F32)).astype(BF16)
        span = pl.ds(k * piece, piece)
        merged.append(send(mrg.at[span], rv.at[2, span], me_f, me_v ^ 4))

    for copy in terms:
        copy.wait()
    total = frs[0].astype(F32)
    for j in range(1, nf):
        total = total + frs[j].astype(F32)
    slab = fl // ny
    red[...] = total.reshape(ny, slab, f_all)
    yr[y] = red[y]
    step = [send(red.at[y ^ d], yr.at[y], me_f, (y ^ d) * NZ + z) for d in range(1, ny)]
    relay(0)
    for copy in step:
        copy.wait()
    total = yr[0]
    for j in range(1, ny):
        total = total + yr[j]
    hr, hc = slab // 2, f_all // 2
    for q in range(4):
        zs[q] = total[q // 2 * hr : (q // 2 + 1) * hr, q % 2 * hc : (q % 2 + 1) * hc]
    zr[zl] = zs[zl]
    step = [send(zs.at[zl ^ d], zr.at[zl], me_f, me_v ^ d) for d in range(1, 4)]
    relay(1)
    for copy in step:
        copy.wait()
    zsum[...] = zr[0] + zr[1] + zr[2] + zr[3]
    zh[zhi] = zsum[...]
    step = [send(zsum, zh.at[zhi], me_f, me_v ^ (4 * d)) for d in range(1, 4)]
    relay(2)
    for copy in step:
        copy.wait()
    zag[zl] = zh[0] + zh[1] + zh[2] + zh[3]
    step = [send(zag.at[zl], zag.at[zl], me_f, me_v ^ d) for d in range(1, 4)]
    relay(3)
    for copy in step:
        copy.wait()
    for q in range(4):
        yag[y, q // 2 * hr : (q // 2 + 1) * hr, q % 2 * hc : (q % 2 + 1) * hc] = zag[q]
    step = [send(yag.at[y], yag.at[y], me_f, (y ^ d) * NZ + z) for d in range(1, ny)]
    for copy in step:
        copy.wait()
    wgrad[me_f] = yag[...].reshape(fl, f_all)
    step = [
        send(wgrad.at[me_f], wgrad.at[me_f], me_f ^ (2 * d), me_v) for d in range(1, nf // 2)
    ]
    last = [send(wgrad.at[me_f], wgrad.at[me_f], me_f ^ 1, me_v)]
    for d, copy in enumerate(step, 1):
        copy.wait()
        other = me_f ^ (2 * d)
        last.append(send(wgrad.at[other], wgrad.at[other], me_f ^ 1, me_v))
    for copy in waits:
        copy.wait()
    for k in range(CHUNKS):
        merged[k].wait()
        for t in range(k * piece, (k + 1) * piece):
            sums = summed(0, t) + rv[0, t].astype(F32) + rv[1, t].astype(F32)
            fgrad[:, t * tile : (t + 1) * tile] = (sums + rv[2, t].astype(F32)).astype(BF16)
    for copy in last:
        copy.wait()


def body(features, tiles, tile_rows, tile_cols, tile_counts, weight, output_gradient):
    fl, vdev = features.shape
    slots, tile = tiles.shape[1], tiles.shape[2]
    row_tiles = vdev // tile
    nf, nv = lax.axis_size("feat"), lax.axis_size("vert")
    ny = nv // NZ
    f_all, share = output_gradient.shape
    smem = pl.BlockSpec(memory_space=pltpu.SMEM)
    vmem = pl.BlockSpec(memory_space=pltpu.VMEM)
    index = pl.pallas_call(
        functools.partial(index_kernel, slots, row_tiles),
        out_shape=jax.ShapeDtypeStruct((offsets(slots, row_tiles)[-1],), jnp.int32),
        in_specs=[smem] * 3,
        out_specs=smem,
    )(tile_rows, tile_cols, tile_counts)
    slab = fl // ny
    copies = 2 * (2 + 2 * CHUNKS) + 3 * (nf - 1) + 2 * (ny - 1) + 9 + (nf // 2 - 1) + nf // 2
    scratch = [
        ((LEVELS + 1) * row_tiles, fl, tile, BF16),
        (slots + 1, fl, tile, F32),
        (f_all, f_all, BF16),
        (nf, fl, share, BF16),
        (nf, fl, share, BF16),
        (f_all, share, BF16),
        (nf, row_tiles // nf, fl, tile, BF16),
        (row_tiles, fl, tile, BF16),
        (nf, fl, f_all, BF16),
        (nf, fl, f_all, BF16),
        (ny, slab, f_all, F32),
        (ny, slab, f_all, F32),
        (4, slab // 2, f_all // 2, F32),
        (4, slab // 2, f_all // 2, F32),
        (slab // 2, f_all // 2, F32),
        (4, slab // 2, f_all // 2, F32),
        (4, slab // 2, f_all // 2, F32),
        (ny, slab, f_all, F32),
        (3, row_tiles, fl, tile, BF16),
        (row_tiles, fl, tile, BF16),
        (row_tiles, fl, tile, BF16),
        (3, row_tiles, fl, tile, BF16),
    ]
    act, wgrad, fgrad = pl.pallas_call(
        functools.partial(layer_kernel, nf, ny, slots, row_tiles, tile),
        out_shape=(
            jax.ShapeDtypeStruct((f_all, share), BF16),
            jax.ShapeDtypeStruct((nf, fl, f_all), F32),
            jax.ShapeDtypeStruct((fl, vdev), BF16),
        ),
        in_specs=[smem] + [vmem] * 4,
        out_specs=(vmem, vmem, vmem),
        scratch_shapes=[pltpu.VMEM(s[:-1], s[-1]) for s in scratch]
        + [pltpu.SemaphoreType.DMA((copies,)), pltpu.SemaphoreType.DMA((copies,))],
        compiler_params=pltpu.CompilerParams(
            collective_id=0, has_side_effects=True, vmem_limit_bytes=40 * 1024 * 1024
        ),
    )(index, features, tiles[0], weight, output_gradient)
    return act, wgrad.reshape(f_all, f_all), fgrad


def solution(mesh):
    in_specs = (
        P("feat", "vert"),
        P("vert", None, None, None),
        P("vert", None),
        P("vert", None),
        P("vert"),
        P(),
        P(None, ("vert", "feat")),
    )
    out_specs = (P(None, ("vert", "feat")), P(), P("feat", "vert"))
    return jax.shard_map(body, mesh=mesh, in_specs=in_specs, out_specs=out_specs, check_vma=False)
```

time: 630 us -> 142 us (0.23)
  waiting for transfers between devices: 525 us -> 0 us
  Pallas kernels: 0 us -> 133 us
  starting transfers between devices: 53.5 us -> 0 us
  local copies, waits for them, and re-layouts: 22.5 us -> 7.49 us
  between operations: 14.9 us -> 1.31 us
  matrix products: 7.74 us -> 0 us
    psum x1 -> x0, waiting for transfers between devices: 436 us -> none  [body(): weight_gradient = lax.psum(weight_term, ('feat', 'vert'))]
    pallas_call x0 -> x2, Pallas kernels: none -> 133 us  [the longest x1 129 us: body(): pl.pallas_call(functools.partial(layer_kernel, nf, ny, slots, row_tiles,...]
    ppermute x8 -> x0, waiting for transfers between devices: 75.5 us -> none  [partner(): lax.ppermute(shard, axis, [(i, i ^ 1 << stride) for i in range(lax.axis_s...]
    ppermute x8 -> x0, starting transfers between devices: 44.3 us -> none  [partner(): lax.ppermute(shard, axis, [(i, i ^ 1 << stride) for i in range(lax.axis_s...]
    all_to_all x2 -> x0, waiting for transfers between devices: 12.8 us -> none  [the longest x1 6.48 us: body(): lax.all_to_all(agg_grad, 'feat', split_axis=0, concat_axis=1, tiled=True)]
    all_to_all x2 -> x0, starting transfers between devices: 9.15 us -> none  [the longest x1 4.79 us: body(): lax.all_to_all(aggregated, 'feat', split_axis=1, concat_axis=0, tiled=True)]
    dot_general x7 -> x0, matrix products: 7.74 us -> none  [the longest x1 2.37 us: position_summands(): jnp.einsum('sc,cfk->fsk', placing, share_value)]
  transfers between devices with their start and end apart: 11 -> 0, of which waited for: 6 -> 0; matrix products, arithmetic and copies ran while one was open for 1% -> 0% of each run, Pallas kernels for 0% -> 0%
where the time goes in v1:
time: 142 us; the launch traced here: 141 us
  Pallas kernels  133 us (94%)
  local copies, waits for them, and re-layouts  7.49 us (5%)
    pallas_call x1, Pallas kernels, body(): pl.pallas_call(functools.partial(layer_kernel, nf, ny, slots, row_tiles,...  129 us
    unnamed x13, local copies, waits for them, and re-layouts  7.49 us
    pallas_call x1, Pallas kernels, body(): pl.pallas_call(functools.partial(index_kernel, slots, row_tiles), out_sha...  3.62 us

profile of v1, /device:TPU:1, one launch (start us, length us, event | category | flops | bytes accessed | tf_op | source)
XLA Modules:
  0.0 141.5 jit_solution(4703266595939615466)
XLA Ops:
  1.3 3.6 %shard_map.94.idx = s32[320]{0:T(512)} custom-call(s32[1,56]{1,0:T(1,128)} %rows_ref.1, s32[1,56]{1,0:T(1,128)} %cols_ref.1, s32[1]{0:T(128)S(6)} %copy.13.count_ref), custom_call_target="tpu_custom_call" | custom-call | tf_op jit(solution)/shard_map/pallas_call | solution.py:282
  4.9 0.0 copy-start
  4.9 1.5 %copy-done = bf16[1,56,128,128]{3,2,1,0:T(8,128)(2,1)S(1)} copy-done((bf16[1,56,128,128]{3,2,1,0:T(8,128)(2,1)S(1)}, bf16[1,56,128,128]{3,2,1,0:T(8,128)(2,1)}, u32[]{:S(2)}) %copy-start) | copy-done | bytes 1835032
  6.4 0.0 copy-start.1
  6.4 1.0 copy-done.1
  7.4 0.0 copy-start.2
  7.4 0.9 copy-done.2
  8.4 0.0 copy-start.3
  8.4 0.9 copy-done.3
  9.3 0.0 copy-start.4
  9.3 0.7 copy-done.4
  10.0 129.0 %shard_map.95 = (bf16[512,256]{1,0:T(8,128)(2,1)S(1)}, f32[8,64,512]{2,1,0:T(8,128)S(1)}, bf16[64,2048]{1,0:T(8,128)(2,1)S(1)}) custom-call(s32[320]{0:T(512)S(1)} %copy-done.4, bf16[64,2048]{1,0:T(8,128)(2,1)S(1)} %copy-done.2, bf16[56,128,128]{2,1,0:T(8,128)(2,1)S(1)} %bitcast.2, bf16[512,512]{1,0:T(8,128)(2,1)S(1)} %copy-done.1, ...), custom_call_target="tpu_custom_call" | custom-call | tf_op jit(solution)/shard_map/pallas_call | solution.py:314
  139.1 0.7 copy.14
  139.8 1.0 copy.15
  140.8 0.7 copy.16
Async XLA Ops:
  4.9 1.5 %copy-start = (bf16[1,56,128,128]{3,2,1,0:T(8,128)(2,1)S(1)}, bf16[1,56,128,128]{3,2,1,0:T(8,128)(2,1)}, u32[]{:S(2)}) copy-start(bf16[1,56,128,128]{3,2,1,0:T(8,128)(2,1)} %param.8) | copy-start | bytes 5505028
  6.4 1.0 copy-start.1
  7.4 0.9 copy-start.2
  8.4 0.9 copy-start.3
  9.3 0.7 copy-start.4

commit v2 on v0

v2 whole, which is shorter than its diff:
```python
import functools

import jax
import jax.numpy as jnp
from jax import lax
from jax.experimental import pallas as pl
from jax.experimental.pallas import tpu as pltpu
from jax.sharding import PartitionSpec as P

NZ = 16
LEVELS = 4
HALVES = 2
CHUNKS = 4
ORDER = (
    ("products", 0),
    ("near", 0),
    ("products", 1),
    ("scatter",),
    ("far", 0),
    ("near", 1),
    ("relay", 1),
    ("gather",),
    ("far", 1),
    ("relay", 2),
    ("spread",),
    ("relay", 1),
    ("pass",),
)
BACK = 2
GROUP = 8
SRC, ROW, PREV_F, PREV_B, LAST_F, LAST_B = range(6)
LANES = 128
MESH = pl.DeviceIdType.MESH
BF16, F32, I32 = jnp.bfloat16, jnp.float32, jnp.int32
NT = (((1,), (1,)), ((), ()))


def index_table(slots, row_tiles, rows, cols, count, table):
    across = lax.broadcasted_iota(I32, (slots, slots), 1)
    down = lax.broadcasted_iota(I32, (slots, slots), 0)
    wide = lax.broadcasted_iota(I32, (slots, LANES), 1)
    deep = lax.broadcasted_iota(I32, (slots, LANES), 0)
    valid = lax.broadcasted_iota(I32, (1, slots), 1) < count
    shift = row_tiles.bit_length() - 1
    differ = lax.shift_right_arithmetic(cols, shift) ^ lax.axis_index("vert")
    level = jnp.zeros(cols.shape, I32)
    for bit in range(LEVELS):
        level = level + jnp.where(differ >= (1 << bit), 1, 0).astype(I32)
    target = jnp.where(valid, level * row_tiles + (cols & (row_tiles - 1)), 0)
    line = jnp.where(valid, rows, 0)
    table[SRC : SRC + 1, :slots] = target
    table[ROW : ROW + 1, :slots] = line
    for key, prev_at, last_at in ((line, PREV_F, LAST_F), (target, PREV_B, LAST_B)):
        key = jnp.where(valid, key, -1)
        column = jnp.max(jnp.where(across == down, key, -1), axis=1, keepdims=True)
        same = (column == key) & (down < across) & (column >= 0)
        before = jnp.max(jnp.where(same, down, -1), axis=0, keepdims=True)
        table[prev_at : prev_at + 1, :slots] = jnp.where(before < 0, slots, before)
        final = jnp.max(jnp.where(column == wide, deep, -1), axis=0, keepdims=True)
        table[last_at : last_at + 1, :] = jnp.where(final < 0, slots, final)


def layer_kernel(
    nf, ny, slots, row_tiles, tile,
    counts, rows_in, cols_in, feat_in, tiles_in, weight_in, grad_in,
    act, wgrad, fgrad,
    table, feat, tiles, weight, out_grad,
    stk0, stk1, acc, wt, agg, full, pg, ag, gc0, gc1, wgs, frs, zs, zr, zag, total_of, pag,
    part, rly, mrg, rv, idx, lsem, ssem, rsem,
):
    stk, gc = (stk0, stk1), (gc0, gc1)
    fl = feat.shape[0]
    f_all = nf * fl
    hl = fl // HALVES
    per = row_tiles // nf
    share = per * tile
    me_f, me_v = lax.axis_index("feat"), lax.axis_index("vert")
    z, y = me_v % NZ, me_v // NZ
    piece, bpiece = row_tiles // CHUNKS, row_tiles // BACK

    used = [0]

    def send(source, dest, f, v):
        n = used[0]
        used[0] += 1
        copy = pltpu.make_async_remote_copy(
            source, dest, ssem.at[n], rsem.at[n], device_id=(f, v), device_id_type=MESH
        )
        copy.start()
        return copy

    def fetch(source, dest, n):
        copy = pltpu.make_async_copy(source, dest, lsem.at[n])
        copy.start()
        return copy

    peers = [(me_f, me_v ^ d) for d in range(NZ - 1, 0, -1)]
    plane = [(df, dy) for df in range(nf) for dy in range(ny) if df or dy]
    peers += [(me_f ^ df, (y ^ dy) * NZ + z) for df, dy in plane]
    barrier = pltpu.get_barrier_semaphore()
    for f, v in peers:
        pl.semaphore_signal(barrier, inc=1, device_id=(f, v), device_id_type=MESH)
    get_feat = fetch(feat_in, feat, 0)
    get_weight = fetch(weight_in, weight, 1)
    get_tiles = fetch(tiles_in, tiles, 2)
    get_grad = fetch(grad_in, out_grad, 3)
    get_feat.wait()
    for hf in range(HALVES):
        for t in range(row_tiles):
            stk[hf][t] = feat[hf * hl : (hf + 1) * hl, t * tile : (t + 1) * tile]
    pl.semaphore_wait(barrier, len(peers))

    def span_of(level, k):
        return pl.ds(level * row_tiles + k * piece, piece)

    def start_features(hf):
        first = [
            send(stk[hf].at[span_of(0, k)], stk[hf].at[span_of(3, k)], me_f, me_v ^ 4)
            for k in range(CHUNKS)
        ]
        direct = [
            send(
                stk[hf].at[pl.ds(0, row_tiles)],
                stk[hf].at[pl.ds((bit + 1) * row_tiles, row_tiles)],
                me_f,
                me_v ^ (1 << bit),
            )
            for bit in (1, 0)
        ]
        return first, direct

    def hand_on(hf, first):
        handed = []
        for k, copy in enumerate(first):
            copy.wait()
            handed.append(send(stk[hf].at[span_of(3, k)], stk[hf].at[span_of(4, k)], me_f, me_v ^ 12))
        return handed

    def chain(out, picked, use_nt, prev):
        def some(g, carry):
            products = []
            for u in range(GROUP):
                c = g * GROUP + u
                if use_nt:
                    products.append(
                        lax.dot_general(picked(c), tiles[0, c], NT, preferred_element_type=F32)
                    )
                else:
                    products.append(jnp.dot(picked(c), tiles[0, c], preferred_element_type=F32))
            for u in range(GROUP):
                c = g * GROUP + u
                out[c] = products[u] + out[idx[prev, c]]
            return carry

        lax.fori_loop(0, slots // GROUP, some, 0)

    def aggregate(hf):
        chain(acc.at[hf], lambda c: stk[hf][idx[SRC, c]], True, PREV_F)
        for r in range(row_tiles):
            k = r % per
            agg[hf, r // per, :, k * tile : (k + 1) * tile] = acc[hf, idx[LAST_F, r]].astype(BF16)
        full[hf, me_f] = agg[hf, me_f]
        return [
            send(agg.at[hf, me_f ^ d], full.at[hf, me_f], me_f ^ d, me_v) for d in range(1, nf)
        ]

    first, direct = start_features(0)
    index_table(slots, row_tiles, rows_in[...], cols_in[...], counts[0], table)
    get_index = fetch(table, idx, 4)
    for hf in range(HALVES):
        acc[hf, slots] = jnp.zeros(acc.shape[2:], F32)
    get_weight.wait()
    for hf in range(HALVES):
        mine = weight[...].reshape(nf, HALVES, hl, f_all)[:, hf].reshape(f_all // HALVES, f_all)
        wt[hf] = mine.astype(F32).T.astype(BF16)
    get_index.wait()
    get_tiles.wait()
    get_grad.wait()
    moves = []
    for hf in range(HALVES):
        handed = hand_on(hf, first)
        arrivals = direct + handed
        if hf + 1 < HALVES:
            first, direct = start_features(hf + 1)
        for copy in arrivals:
            copy.wait()
        moves.append(aggregate(hf))

    blocks = 2
    block = f_all // blocks
    for hf in range(HALVES):
        for copy in moves[hf]:
            copy.wait()
    rows = [full[hf].reshape(f_all // HALVES, share) for hf in range(HALVES)]
    for i in range(blocks):
        at = slice(i * block, (i + 1) * block)
        pre = jnp.dot(wt[0, at, :], rows[0], preferred_element_type=F32)
        for hf in range(1, HALVES):
            pre = pre + jnp.dot(wt[hf, at, :], rows[hf], preferred_element_type=F32)
        sigma = jax.nn.sigmoid(pre)
        act[at, :] = (pre * sigma).astype(BF16)
        pg[at, :] = (
            out_grad[at, :].astype(F32) * sigma * (1.0 + pre * (1.0 - sigma))
        ).astype(BF16)
    grads = pg[...]
    mine = pl.ds(me_f * per, per)
    back = []
    for hf in range(HALVES):
        own = weight[...].reshape(nf, HALVES, hl, f_all)[:, hf].reshape(f_all // HALVES, f_all)
        agg_grad = jnp.dot(own, grads, preferred_element_type=F32).astype(BF16)
        for k in range(per):
            ag[hf, :, k] = agg_grad[:, k * tile : (k + 1) * tile].reshape(nf, hl, tile)
        back.append(
            [send(ag.at[hf, me_f ^ d], gc[hf].at[mine], me_f ^ d, me_v) for d in range(1, nf)]
        )
        gc[hf][mine] = ag[hf, me_f]
    for hf in range(HALVES):
        term = lax.dot_general(rows[hf], grads, NT, preferred_element_type=F32).astype(BF16)
        wgs[:, hf * hl : (hf + 1) * hl, :] = term.reshape(nf, hl, f_all)
    slab = fl // ny
    me_p = me_f * ny + y
    terms = [
        send(
            wgs.at[me_f ^ df, pl.ds((y ^ dy) * slab, slab)],
            frs.at[me_p],
            me_f ^ df,
            (y ^ dy) * NZ + z,
        )
        for df, dy in plane
    ]
    frs[me_p] = wgs[me_f, pl.ds(y * slab, slab)]

    def summed(hf, level, t):
        return acc[hf, idx[LAST_B, level * row_tiles + t]]

    direct, relayed, merged, last, steps = [], [], [], [], {}
    hr, hc = slab // 4, f_all // 4
    parts = [
        (slice(q // 4 * hr, (q // 4 + 1) * hr), slice(q % 4 * hc, (q % 4 + 1) * hc))
        for q in range(NZ)
    ]
    same_core = [(df, dy) for df, dy in plane if df % 2 == 0]

    def products(hf):
        for copy in back[hf]:
            copy.wait()
        chain(acc.at[hf], lambda c: gc[hf][idx[ROW, c]], False, PREV_B)

    def far(hf):
        for k in range(BACK):
            for t in range(k * bpiece, (k + 1) * bpiece):
                part[hf, 2, t] = summed(hf, 4, t).astype(BF16)
            span = pl.ds(k * bpiece, bpiece)
            relayed.append(send(part.at[hf, 2, span], rly.at[hf, span], me_f, me_v ^ 12))

    def near(hf):
        for bit in (1, 0):
            for t in range(row_tiles):
                part[hf, bit, t] = summed(hf, bit + 1, t).astype(BF16)
            direct.append(send(part.at[hf, bit], rv.at[hf, bit], me_f, me_v ^ (1 << bit)))

    def relay(count):
        for n in range(len(merged), len(merged) + count):
            hf, k = divmod(n, BACK)
            relayed[n].wait()
            for t in range(k * bpiece, (k + 1) * bpiece):
                mrg[hf, t] = (summed(hf, 3, t) + rly[hf, t].astype(F32)).astype(BF16)
            span = pl.ds(k * bpiece, bpiece)
            merged.append(send(mrg.at[hf, span], rv.at[hf, 2, span], me_f, me_v ^ 4))

    def scatter():
        for copy in terms:
            copy.wait()
        total = frs[0].astype(F32)
        for p in range(1, nf * ny):
            total = total + frs[p].astype(F32)
        for q, (at_r, at_c) in enumerate(parts):
            zs[q] = total[at_r, at_c]
        zr[z] = zs[z]
        steps["z"] = [send(zs.at[z ^ d], zr.at[z], me_f, me_v ^ d) for d in range(NZ - 1, 0, -1)]

    def gather():
        for copy in steps["z"]:
            copy.wait()
        total = zr[0]
        for q in range(1, NZ):
            total = total + zr[q]
        zag[z] = total
        steps["z"] = [send(zag.at[z], zag.at[z], me_f, me_v ^ d) for d in range(NZ - 1, 0, -1)]

    def spread():
        for copy in steps["z"]:
            copy.wait()
        for q, (at_r, at_c) in enumerate(parts):
            total_of[at_r, at_c] = zag[q]
        pag[me_p] = total_of[...].astype(BF16)
        steps["p"] = [
            send(pag.at[me_p], pag.at[me_p], me_f ^ df, (y ^ dy) * NZ + z) for df, dy in same_core
        ]
        last.append(send(pag.at[me_p], pag.at[me_p], me_f ^ 1, me_v))

    def pass_over():
        for (df, dy), copy in zip(same_core, steps["p"]):
            copy.wait()
            other = (me_f ^ df) * ny + (y ^ dy)
            last.append(send(pag.at[other], pag.at[other], me_f ^ 1, me_v))

    for name, *args in ORDER:
        {
            "products": products, "far": far, "near": near, "relay": relay, "scatter": scatter,
            "gather": gather, "spread": spread, "pass": pass_over,
        }[name](*args)
    for copy in direct + merged:
        copy.wait()
    for hf in range(HALVES):
        for t in range(row_tiles):
            sums = summed(hf, 0, t)
            for bit in range(3):
                sums = sums + rv[hf, bit, t].astype(F32)
            fgrad[hf * hl : (hf + 1) * hl, t * tile : (t + 1) * tile] = sums.astype(BF16)
    for copy in last:
        copy.wait()
    for f in range(nf):
        wgrad[f] = pag[f * ny : (f + 1) * ny].reshape(fl, f_all).astype(F32)


def body(features, tiles, tile_rows, tile_cols, tile_counts, weight, output_gradient):
    fl, vdev = features.shape
    slots, tile = tiles.shape[1], tiles.shape[2]
    row_tiles = vdev // tile
    nf, nv = lax.axis_size("feat"), lax.axis_size("vert")
    ny = nv // NZ
    f_all, share = output_gradient.shape
    smem = pl.BlockSpec(memory_space=pltpu.SMEM)
    vmem = pl.BlockSpec(memory_space=pltpu.VMEM)
    hbm = pl.BlockSpec(memory_space=pltpu.HBM)
    slab = fl // ny
    hl = fl // HALVES
    copies = HALVES * (4 + 2 * CHUNKS + 2 * BACK + 2 * (nf - 1))
    copies += (nf * ny - 1) + 2 * (NZ - 1) + (nf // 2 * ny - 1) + nf // 2 * ny
    scratch = [
        (8, LANES, I32),
        (fl, vdev, BF16),
        (1, slots, tile, tile, BF16),
        (f_all, f_all, BF16),
        (f_all, share, BF16),
        ((LEVELS + 1) * row_tiles, hl, tile, BF16),
        ((LEVELS + 1) * row_tiles, hl, tile, BF16),
        (HALVES, slots + 1, hl, tile, F32),
        (HALVES, f_all, f_all // HALVES, BF16),
        (HALVES, nf, hl, share, BF16),
        (HALVES, nf, hl, share, BF16),
        (f_all, share, BF16),
        (HALVES, nf, row_tiles // nf, hl, tile, BF16),
        (row_tiles, hl, tile, BF16),
        (row_tiles, hl, tile, BF16),
        (nf, fl, f_all, BF16),
        (nf * ny, slab, f_all, BF16),
        (NZ, slab // 4, f_all // 4, F32),
        (NZ, slab // 4, f_all // 4, F32),
        (NZ, slab // 4, f_all // 4, F32),
        (slab, f_all, F32),
        (nf * ny, slab, f_all, BF16),
        (HALVES, 3, row_tiles, hl, tile, BF16),
        (HALVES, row_tiles, hl, tile, BF16),
        (HALVES, row_tiles, hl, tile, BF16),
        (HALVES, 3, row_tiles, hl, tile, BF16),
    ]
    act, wgrad, fgrad = pl.pallas_call(
        functools.partial(layer_kernel, nf, ny, slots, row_tiles, tile),
        out_shape=(
            jax.ShapeDtypeStruct((f_all, share), BF16),
            jax.ShapeDtypeStruct((nf, fl, f_all), F32),
            jax.ShapeDtypeStruct((fl, vdev), BF16),
        ),
        in_specs=[smem, vmem, vmem] + [hbm] * 4,
        out_specs=(vmem, vmem, vmem),
        scratch_shapes=[pltpu.VMEM(s[:-1], s[-1]) for s in scratch]
        + [
            pltpu.SMEM((8, LANES), I32),
            pltpu.SemaphoreType.DMA((5,)),
            pltpu.SemaphoreType.DMA((copies,)),
            pltpu.SemaphoreType.DMA((copies,)),
        ],
        compiler_params=pltpu.CompilerParams(
            collective_id=0, has_side_effects=True, vmem_limit_bytes=58 * 1024 * 1024
        ),
    )(tile_counts, tile_rows, tile_cols, features, tiles, weight, output_gradient)
    return act, wgrad.reshape(f_all, f_all), fgrad


def solution(mesh):
    in_specs = (
        P("feat", "vert"),
        P("vert", None, None, None),
        P("vert", None),
        P("vert", None),
        P("vert"),
        P(),
        P(None, ("vert", "feat")),
    )
    out_specs = (P(None, ("vert", "feat")), P(), P("feat", "vert"))
    return jax.shard_map(body, mesh=mesh, in_specs=in_specs, out_specs=out_specs, check_vma=False)
```

time: 630 us -> 125 us (0.20)
  the two profiles are of different devices: /device:TPU:1 before, /device:TPU:2 now
where the time goes in v2:
time: 125 us
  Pallas kernels  119 us (95%)
  local copies, waits for them, and re-layouts  4.68 us (4%)
  between operations  1.3 us (1%)
    pallas_call x1, Pallas kernels, body(): pl.pallas_call(functools.partial(layer_kernel, nf, ny, slots, row_tiles,...  119 us
    unnamed x5, local copies, waits for them, and re-layouts  4.68 us

profile of v2, /device:TPU:2, one launch (start us, length us, event | category | flops | bytes accessed | tf_op | source)
XLA Modules:
  0.0 124.8 jit_solution(7843754172828345456)
XLA Ops:
  1.3 118.8 %shard_map.94 = (bf16[512,256]{1,0:T(8,128)(2,1)}, f32[8,64,512]{2,1,0:T(8,128)}, bf16[64,2048]{1,0:T(8,128)(2,1)}) custom-call(s32[1]{0:T(128)S(6)} %copy.13.counts, s32[1,56]{1,0:T(1,128)} %rows_in.1, s32[1,56]{1,0:T(1,128)} %cols_in.1, bf16[64,2048]{1,0:T(8,128)(2,1)} %feat_in.1, bf16[1,56,128,128]{3,2,1,0:T(8,128)(2,1)} %tiles_in.1, ...), custom_call_target="tpu_custom_call" | custom-call | tf_op jit(solution)/shard_map/pallas_call | solution.py:369
  120.1 0.0 copy-start
  120.1 1.7 %copy.14 = bf16[512,256]{1,0:T(8,128)(2,1)} copy(bf16[512,256]{1,0:T(8,128)(2,1)} %get-tuple-element.12) | data formatting | bytes 524288
  121.8 2.3 %copy.15 = f32[512,512]{1,0:T(8,128)} copy(f32[512,512]{1,0:T(8,128)} %bitcast.1) | data formatting | bytes 2097152
  124.0 0.0 copy-done
  124.1 0.7 copy.16
Async XLA Ops:
  120.1 4.0 %copy-start = (bf16[64,2048]{1,0:T(8,128)(2,1)S(1)}, bf16[64,2048]{1,0:T(8,128)(2,1)}, u32[]{:S(2)}) copy-start(bf16[64,2048]{1,0:T(8,128)(2,1)} %get-tuple-element.14) | copy-start | bytes 786436

commit v3 on v2

--- a/solution.py
+++ b/solution.py
@@ -18,15 +18,15 @@
     ("scatter",),
     ("far", 0),
     ("near", 1),
-    ("relay", 1),
+    ("relay", 2),
     ("gather",),
     ("far", 1),
+    ("relay", 4),
+    ("spread",),
     ("relay", 2),
-    ("spread",),
-    ("relay", 1),
     ("pass",),
 )
-BACK = 2
+BACK = 4
 GROUP = 8
 SRC, ROW, PREV_F, PREV_B, LAST_F, LAST_B = range(6)
 LANES = 128
@@ -320,8 +320,13 @@
             fgrad[hf * hl : (hf + 1) * hl, t * tile : (t + 1) * tile] = sums.astype(BF16)
     for copy in last:
         copy.wait()
-    for f in range(nf):
-        wgrad[f] = pag[f * ny : (f + 1) * ny].reshape(fl, f_all).astype(F32)
+    wgrad[...] = pag[...]
+
+
+def results_kernel(act, wgrad, fgrad, act_out, wgrad_out, fgrad_out):
+    act_out[...] = act[...]
+    wgrad_out[...] = wgrad[...].reshape(wgrad_out.shape).astype(F32)
+    fgrad_out[...] = fgrad[...]
 
 
 def body(features, tiles, tile_rows, tile_cols, tile_counts, weight, output_gradient):
@@ -370,7 +375,7 @@
         functools.partial(layer_kernel, nf, ny, slots, row_tiles, tile),
         out_shape=(
             jax.ShapeDtypeStruct((f_all, share), BF16),
-            jax.ShapeDtypeStruct((nf, fl, f_all), F32),
+            jax.ShapeDtypeStruct((nf * ny, slab, f_all), BF16),
             jax.ShapeDtypeStruct((fl, vdev), BF16),
         ),
         in_specs=[smem, vmem, vmem] + [hbm] * 4,
@@ -386,7 +391,16 @@
             collective_id=0, has_side_effects=True, vmem_limit_bytes=58 * 1024 * 1024
         ),
     )(tile_counts, tile_rows, tile_cols, features, tiles, weight, output_gradient)
-    return act, wgrad.reshape(f_all, f_all), fgrad
+    return pl.pallas_call(
+        results_kernel,
+        out_shape=(
+            jax.ShapeDtypeStruct(act.shape, BF16),
+            jax.ShapeDtypeStruct((f_all, f_all), F32),
+            jax.ShapeDtypeStruct(fgrad.shape, BF16),
+        ),
+        in_specs=[vmem] * 3,
+        out_specs=(vmem,) * 3,
+    )(act, wgrad, fgrad)
 
 
 def solution(mesh):

time: 125 us -> 122 us (0.976)
  the two profiles are of different devices: /device:TPU:2 before, /device:TPU:5 now
where the time goes in v3:
time: 122 us
  Pallas kernels  120 us (98%)
  between operations  1.29 us (1%)
    pallas_call x1, Pallas kernels, body(): pl.pallas_call(functools.partial(layer_kernel, nf, ny, slots, row_tiles,...  118 us

profile of v3, /device:TPU:5, one launch (start us, length us, event | category | flops | bytes accessed | tf_op | source)
XLA Modules:
  0.0 121.7 jit_solution(16922026140612297698)
XLA Ops:
  1.3 118.0 %shard_map.94 = (bf16[512,256]{1,0:T(8,128)(2,1)}, bf16[32,16,512]{2,1,0:T(8,128)(2,1)}, bf16[64,2048]{1,0:T(8,128)(2,1)}) custom-call(s32[1]{0:T(128)S(6)} %copy.10.counts, s32[1,56]{1,0:T(1,128)} %rows_in.1, s32[1,56]{1,0:T(1,128)} %cols_in.1, bf16[64,2048]{1,0:T(8,128)(2,1)} %feat_in.1, bf16[1,56,128,128]{3,2,1,0:T(8,128)(2,1)} %tiles_in.1, ...), custom_call_target="tpu_custom_call" | custom-call | tf_op jit(solution)/shard_map/pallas_call | solution.py:374
  119.3 2.4 %shard_map.95 = (bf16[512,256]{1,0:T(8,128)(2,1)}, f32[512,512]{1,0:T(8,128)}, bf16[64,2048]{1,0:T(8,128)(2,1)}) custom-call(bf16[512,256]{1,0:T(8,128)(2,1)} %get-tuple-element.6.act, bf16[32,16,512]{2,1,0:T(8,128)(2,1)} %get-tuple-element.7.wgrad, bf16[64,2048]{1,0:T(8,128)(2,1)} %get-tuple-element.8.fgrad), custom_call_target="tpu_custom_call" | custom-call | tf_op jit(solution)/shard_map/pallas_call | solution.py:394

commit v4 on v3

--- a/solution.py
+++ b/solution.py
@@ -205,7 +205,7 @@
     grads = pg[...]
     mine = pl.ds(me_f * per, per)
     back = []
-    for hf in range(HALVES):
+    def give_back(hf):
         own = weight[...].reshape(nf, HALVES, hl, f_all)[:, hf].reshape(f_all // HALVES, f_all)
         agg_grad = jnp.dot(own, grads, preferred_element_type=F32).astype(BF16)
         for k in range(per):
@@ -214,6 +214,8 @@
             [send(ag.at[hf, me_f ^ d], gc[hf].at[mine], me_f ^ d, me_v) for d in range(1, nf)]
         )
         gc[hf][mine] = ag[hf, me_f]
+
+    give_back(0)
     for hf in range(HALVES):
         term = lax.dot_general(rows[hf], grads, NT, preferred_element_type=F32).astype(BF16)
         wgs[:, hf * hl : (hf + 1) * hl, :] = term.reshape(nf, hl, f_all)
@@ -229,6 +231,8 @@
         for df, dy in plane
     ]
     frs[me_p] = wgs[me_f, pl.ds(y * slab, slab)]
+    for hf in range(1, HALVES):
+        give_back(hf)
 
     def summed(hf, level, t):
         return acc[hf, idx[LAST_B, level * row_tiles + t]]

time: 122 us -> 121 us (level)
  the two profiles are of different devices: /device:TPU:5 before, /device:TPU:44 now
where the time goes in v4:
time: 121 us
  Pallas kernels  120 us (99%)
  between operations  1.29 us (1%)
    pallas_call x1, Pallas kernels, body(): pl.pallas_call(functools.partial(layer_kernel, nf, ny, slots, row_tiles,...  117 us

profile of v4, /device:TPU:44, one launch (start us, length us, event | category | flops | bytes accessed | tf_op | source)
XLA Modules:
  0.0 120.9 jit_solution(9440216738429390835)
XLA Ops:
  1.3 117.2 %shard_map.94 = (bf16[512,256]{1,0:T(8,128)(2,1)}, bf16[32,16,512]{2,1,0:T(8,128)(2,1)}, bf16[64,2048]{1,0:T(8,128)(2,1)}) custom-call(s32[1]{0:T(128)S(6)} %copy.10.counts, s32[1,56]{1,0:T(1,128)} %rows_in.1, s32[1,56]{1,0:T(1,128)} %cols_in.1, bf16[64,2048]{1,0:T(8,128)(2,1)} %feat_in.1, bf16[1,56,128,128]{3,2,1,0:T(8,128)(2,1)} %tiles_in.1, ...), custom_call_target="tpu_custom_call" | custom-call | tf_op jit(solution)/shard_map/pallas_call | solution.py:378
  118.5 2.4 %shard_map.95 = (bf16[512,256]{1,0:T(8,128)(2,1)}, f32[512,512]{1,0:T(8,128)}, bf16[64,2048]{1,0:T(8,128)(2,1)}) custom-call(bf16[512,256]{1,0:T(8,128)(2,1)} %get-tuple-element.6.act, bf16[32,16,512]{2,1,0:T(8,128)(2,1)} %get-tuple-element.7.wgrad, bf16[64,2048]{1,0:T(8,128)(2,1)} %get-tuple-element.8.fgrad), custom_call_target="tpu_custom_call" | custom-call | tf_op jit(solution)/shard_map/pallas_call | solution.py:398
